TPU v7x, 512 devices: a whole 4x8x8 slice. The times are simulated.
512 devices in a mesh: row: 8 (over z), col: 16 (over y, core), layer: 4 (over x).
Axes of the slice: x: 4, y: 8, z: 8, core: 2. Of those that a mesh axis runs over, the one named last changes fastest.
Arguments:
- panel_values: bfloat16 [16384, 8192], P('row', ('layer', 'col')), may hold values from -6 to 6
- slab_values: bfloat16 [8192, 6144], P(('layer', 'row'), 'col'), may hold values from -0.09375 to 0.09375
- pattern_panel: int32 [128, 64], P('row', ('layer', 'col')), may hold values from 0 to 1, as said below
- pattern_result: int32 [128, 48], P(('row', 'layer'), 'col'), may hold values 0 or 1
Outputs:
- product_slab: bfloat16 [16384, 6144], P(('row', 'layer'), 'col')
Inputs may be any that keep to these rules, and one draw needn't show every extreme that they name: `pattern_panel`: in every group of 16 blocks that one device holds of one block column (block rows r * 16 to r * 16 + 15), 1 to 8 are 1; some group reaches this bound: every group of block column 0 has exactly 8.
All inputs are finite; a program needn't handle non-finite values. No bound on the sum of `pattern_result` on one device may be relied on, other than what follows from the above.
Results may differ from a plain program's by a relative error of at most 0.001.
Values may be sent and summed in bfloat16 or wider, within the bound.
A program may use at most 64 MiB of HBM per device.

v0:
```python
import jax
import jax.numpy as jnp
from jax import lax
from jax.sharding import PartitionSpec as P


def per_device(panel_values, slab_values, pattern_panel, pattern_result):
    block = panel_values.shape[1]
    row_blocks = pattern_panel.shape[0]
    gathered = lax.all_gather(slab_values, "row", axis=0, tiled=True)
    flags = pattern_panel[:, 0]
    blocks_here = panel_values.reshape(row_blocks, block, block)
    masked = (blocks_here * flags.astype(jnp.bfloat16)[:, None, None]).reshape(
        row_blocks * block, block
    )
    partial_value = jnp.dot(
        lax.all_gather(masked, "col", axis=1, tiled=True),
        gathered,
        preferred_element_type=jnp.float32,
    )
    shares = lax.psum_scatter(partial_value, "layer", scatter_dimension=0, tiled=True)
    out_blocks = pattern_result.shape[0]
    col_blocks = pattern_result.shape[1]
    keeper = pattern_result.astype(jnp.float32)
    filtered = shares.reshape(out_blocks, block, col_blocks, block) * keeper[:, None, :, None]
    return filtered.reshape(shares.shape).astype(jnp.bfloat16)


def solution(mesh):
    placed = (
        P("row", ("layer", "col")),
        P(("layer", "row"), "col"),
        P("row", ("layer", "col")),
        P(("row", "layer"), "col"),
    )
    return jax.shard_map(
        per_device,
        mesh=mesh,
        in_specs=placed,
        out_specs=P(("row", "layer"), "col"),
        check_vma=False,
    )
```

profile of v0, /device:TPU:1, one launch (start us, length us, event | category | flops | bytes accessed | tf_op | source)
XLA Modules:
  0.0 186.3 jit_solution(16902584694863488766)
XLA Ops:
  6.5 0.0 all-gather.5.cloned.1.call-start
  6.5 0.7 all-gather.5.cloned.1.call-update
  7.3 0.0 all-gather.3.cloned.1.call-start
  7.3 0.7 convert_bitcast_fusion
  8.0 0.1 broadcast_bitcast_fusion
  8.0 2.2 %broadcast_multiply_fusion = bf16[2048,128]{1,0:T(8,128)(2,1)} fusion(bf16[2048,128]{1,0:T(8,128)(2,1)} %param.4, bf16[2048]{0:T(1024)(128)(2,1)S(1)} %broadcast_bitcast_fusion), kind=kLoop, calls=%fused_computation.2 | loop fusion | flops 262144 | bytes 1052672 | tf_op jit(solution)/shard_map/mul | solution.py:13
  10.3 0.0 all-gather.3.cloned.1.call-update
  10.3 0.0 reduce-scatter.2.cloned.1.call-start
  10.3 44.2 %all-gather.5.cloned.1.call-done = bf16[2048,384]{1,0:T(8,128)(2,1)} async-done(((bf16[256,384]{1,0:T(8,128)(2,1)}), bf16[2048,384]{1,0:T(8,128)(2,1)}) %all-gather.5.cloned.1.call-update) | async-done | bytes 1572880 | tf_op jit(solution)/shard_map/all_gather | solution.py:10
  54.5 73.2 %all-gather.3.cloned.1.call-done = bf16[2048,2048]{1,0:T(8,128)(2,1)} async-done(((bf16[2048,128]{1,0:T(8,128)(2,1)}), bf16[2048,2048]{1,0:T(8,128)(2,1)}) %all-gather.3.cloned.1.call-update) | async-done | bytes 8388624 | tf_op jit(solution)/shard_map/all_gather | solution.py:17
  127.7 10.1 %fusion = f32[2048,384]{1,0:T(8,128)} fusion(bf16[2048,2048]{1,0:T(8,128)(2,1)} %all-gather.3.cloned.1.call-done, bf16[2048,384]{1,0:T(8,128)(2,1)} %all-gather.5.cloned.1.call-done), kind=kOutput, calls=%fused_computation.5 | convolution fusion | flops 3221225472 | bytes 13107200 | tf_op jit(solution)/shard_map/dot_general | solution.py:16
  137.8 0.0 copy-start
  137.8 0.0 reduce-scatter.2.cloned.1.call-update
  137.8 0.7 copy-done
  138.4 0.1 copy.5
  138.5 0.2 mul.28
  138.7 0.1 copy.9
  138.8 0.3 copy.6
  139.1 38.8 %reduce-scatter.2.cloned.1.call-done = f32[512,384]{1,0:T(8,128)} async-done(((f32[2048,384]{1,0:T(8,128)}), f32[512,384]{1,0:T(8,128)}) %reduce-scatter.2.cloned.1.call-update) | async-done | bytes 786448 | tf_op jit(solution)/shard_map/reduce_scatter | solution.py:21
  177.8 2.0 %multiply_convert_fusion = bf16[512,384]{1,0:T(8,128)(2,1)} fusion(f32[512,384]{1,0:T(8,128)} %reduce-scatter.2.cloned.1.call-done, f32[512,384]{1,0:T(8,128)S(1)} %copy.6), kind=kLoop, calls=%fused_computation.1 | loop fusion | flops 393216 | bytes 1966080 | tf_op jit(solution)/shard_map/convert_element_type | solution.py:26
  (1 shorter events, 0.0 us)
Async XLA Ops:
  6.5 48.0 %all-gather.5.cloned.1.call-start = ((), (), s32[]{:S(2)}) async-start(), calls=%async_computation.2 | async-start | bytes 1769472 | tf_op jit(solution)/shard_map/all_gather | solution.py:10
  7.3 120.5 %all-gather.3.cloned.1.call-start = ((), (), s32[]{:S(2)}) async-start(), calls=%async_computation.1 | async-start | bytes 8912896 | tf_op jit(solution)/shard_map/all_gather | solution.py:17
  10.3 167.5 %reduce-scatter.2.cloned.1.call-start = ((), (), s32[]{:S(2)}) async-start(), calls=%async_computation.3 | async-start | bytes 3932160 | tf_op jit(solution)/shard_map/reduce_scatter | solution.py:21
  137.8 0.7 copy-start
Sparse Core Ops, SparseCore 0:
  9.4 45.0 all-gather.4
  56.6 71.0 all-gather.2
  137.9 39.8 reduce-scatter.1
where the time goes:
time: 187 us; the launch traced here: 186 us
  waiting for transfers between devices  157 us (84%)
  between operations  13.1 us (7%)
  matrix products  10.1 us (5%)
  other arithmetic  4.83 us (3%)
    all_gather x1, waiting for transfers between devices, per_device(): lax.all_gather(masked, 'col', axis=1, tiled=True)  73.2 us
    all_gather x1, waiting for transfers between devices, per_device(): gathered = lax.all_gather(slab_values, 'row', axis=0, tiled=True)  44.2 us
    reduce_scatter x1, waiting for transfers between devices, per_device(): lax.psum_scatter(partial_value, 'layer', scatter_dimension=0, tiled=True)  38.8 us
    dot_general x1, matrix products, per_device(): jnp.dot(lax.all_gather(masked, 'col', axis=1, tiled=True), gathered, pref...  10.1 us
  transfers between devices with their start and end apart: 3, of which 3 were waited for; matrix products, arithmetic and copies ran while one was open for 2% of the time, Pallas kernels for 0%

commit v1 on v0

--- a/solution.py
+++ b/solution.py
@@ -14,7 +14,9 @@
         row_blocks * block, block
     )
     partial_value = jnp.dot(
-        lax.all_gather(masked, "col", axis=1, tiled=True),
+        jnp.concatenate(
+            lax.all_to_all(jnp.stack([masked] * lax.axis_size("col")), "col", 0, 0), axis=1
+        ),
         gathered,
         preferred_element_type=jnp.float32,
     )

time: 187 us -> 271 us (1.45)
  waiting for transfers between devices: 157 us -> 226 us
  starting transfers between devices: 0.08 us -> 11.4 us
  local copies, waits for them, and re-layouts: 1.31 us -> 5.85 us
    all_to_all x0 -> x1, waiting for transfers between devices: none -> 140 us  [per_device(): lax.all_to_all(jnp.stack([masked] * lax.axis_size('col')), 'col', 0, 0)]
    all_gather x1 -> x0, waiting for transfers between devices: 73.2 us -> none  [per_device(): lax.all_gather(masked, 'col', axis=1, tiled=True)]
    all_to_all x0 -> x1, starting transfers between devices: none -> 11.3 us  [per_device(): lax.all_to_all(jnp.stack([masked] * lax.axis_size('col')), 'col', 0, 0)]
    another operation x0 -> x1, local copies, waits for them, and re-layouts: none -> 4.32 us  [per_device(): jnp.stack([masked] * lax.axis_size('col'))]
    reduce_scatter x1, waiting for transfers between devices: 38.8 us -> 42.1 us  [per_device(): lax.psum_scatter(partial_value, 'layer', scatter_dimension=0, tiled=True)]
  transfers between devices with their start and end apart: 3 -> 3, of which waited for: 3 -> 3; matrix products, arithmetic and copies ran while one was open for 2% -> 0% of each run, Pallas kernels for 0% -> 0%
where the time goes in v1:
time: 271 us; the launch traced here: 270 us
  waiting for transfers between devices  226 us (83%)
  between operations  13.4 us (5%)
  starting transfers between devices  11.4 us (4%)
  matrix products  10.1 us (4%)
  local copies, waits for them, and re-layouts  5.85 us (2%)
  other arithmetic  3.99 us (1%)
    all_to_all x1, waiting for transfers between devices, per_device(): lax.all_to_all(jnp.stack([masked] * lax.axis_size('col')), 'col', 0, 0)  140 us
    all_gather x1, waiting for transfers between devices, per_device(): gathered = lax.all_gather(slab_values, 'row', axis=0, tiled=True)  43.1 us
    reduce_scatter x1, waiting for transfers between devices, per_device(): lax.psum_scatter(partial_value, 'layer', scatter_dimension=0, tiled=True)  42.1 us
    all_to_all x1, starting transfers between devices, per_device(): lax.all_to_all(jnp.stack([masked] * lax.axis_size('col')), 'col', 0, 0)  11.3 us
    dot_general x1, matrix products, per_device(): jnp.dot(jnp.concatenate(lax.all_to_all(jnp.stack([masked] * lax.axis_size...  10.1 us
  transfers between devices with their start and end apart: 3, of which 3 were waited for; matrix products, arithmetic and copies ran while one was open for 0% of the time, Pallas kernels for 0%

profile of v1, /device:TPU:1, one launch (start us, length us, event | category | flops | bytes accessed | tf_op | source)
XLA Modules:
  0.0 270.4 jit_solution(9229839142298473458)
XLA Ops:
  6.5 0.7 convert_bitcast_fusion
  7.2 0.1 broadcast_bitcast_fusion
  7.3 1.4 broadcast_multiply_fusion
  8.6 0.2 copy.5
  8.9 4.3 %stack.3 = bf16[16,2048,128]{1,2,0:T(8,128)(2,1)} broadcast(bf16[2048,128]{0,1:T(8,128)(2,1)S(1)} %copy.5), dimensions={1,2} | broadcast | bytes 8912896 | tf_op jit(solution)/shard_map/stack | solution.py:18
  13.2 11.3 %all-to-all-start = ((bf16[16,2048,128]{1,2,0:T(8,128)(2,1)}), bf16[16,2048,128]{1,2,0:T(8,128)(2,1)}, u32[]{:S(2)}, u32[]{:S(2)}) async-start(bf16[16,2048,128]{1,2,0:T(8,128)(2,1)} %stack.3), calls=%async_computation | async-start | bytes 16777216 | tf_op jit(solution)/shard_map/all_to_all | solution.py:18
  24.5 0.0 all-gather.2.cloned.1.call-start
  24.6 0.7 all-gather.2.cloned.1.call-update
  25.3 0.0 reduce-scatter.2.cloned.1.call-start
  25.3 43.1 %all-gather.2.cloned.1.call-done = bf16[2048,384]{1,0:T(8,128)(2,1)} async-done(((bf16[256,384]{1,0:T(8,128)(2,1)}), bf16[2048,384]{1,0:T(8,128)(2,1)}) %all-gather.2.cloned.1.call-update) | async-done | bytes 1572880 | tf_op jit(solution)/shard_map/all_gather | solution.py:10
  68.4 139.7 %all-to-all-done = bf16[16,2048,128]{1,2,0:T(8,128)(2,1)} async-done(((bf16[16,2048,128]{1,2,0:T(8,128)(2,1)}), bf16[16,2048,128]{1,2,0:T(8,128)(2,1)}, u32[]{:S(2)}, u32[]{:S(2)}) %all-to-all-start) | async-done | bytes 8388640 | tf_op jit(solution)/shard_map/all_to_all | solution.py:18
  208.1 10.1 %fusion = f32[2048,384]{1,0:T(8,128)} fusion(bf16[2048,2048]{0,1:T(8,128)(2,1)} %bitcast.3, bf16[2048,384]{1,0:T(8,128)(2,1)} %all-gather.2.cloned.1.call-done), kind=kOutput, calls=%fused_computation.5 | convolution fusion | flops 3221225472 | bytes 13107200 | tf_op jit(solution)/shard_map/dot_general | solution.py:16
  218.2 0.0 copy-start
  218.2 0.0 reduce-scatter.2.cloned.1.call-update
  218.2 0.7 copy-done
  218.9 0.1 copy.6
  219.0 0.2 mul.29
  219.2 0.1 copy.10
  219.2 0.3 copy.7
  219.5 42.1 %reduce-scatter.2.cloned.1.call-done = f32[512,384]{1,0:T(8,128)} async-done(((f32[2048,384]{1,0:T(8,128)}), f32[512,384]{1,0:T(8,128)}) %reduce-scatter.2.cloned.1.call-update) | async-done | bytes 786448 | tf_op jit(solution)/shard_map/reduce_scatter | solution.py:23
  261.6 2.0 multiply_convert_fusion
  (1 shorter events, 0.0 us)
Async XLA Ops:
  13.2 194.9 %all-to-all-start = ((bf16[16,2048,128]{1,2,0:T(8,128)(2,1)}), bf16[16,2048,128]{1,2,0:T(8,128)(2,1)}, u32[]{:S(2)}, u32[]{:S(2)}) async-start(bf16[16,2048,128]{1,2,0:T(8,128)(2,1)} %stack.3), calls=%async_computation | async-start | bytes 16777216 | tf_op jit(solution)/shard_map/all_to_all | solution.py:18
  24.5 43.9 %all-gather.2.cloned.1.call-start = ((), (), s32[]{:S(2)}) async-start(), calls=%async_computation.2 | async-start | bytes 1769472 | tf_op jit(solution)/shard_map/all_gather | solution.py:10
  25.3 236.3 %reduce-scatter.2.cloned.1.call-start = ((), (), s32[]{:S(2)}) async-start(), calls=%async_computation.3 | async-start | bytes 3932160 | tf_op jit(solution)/shard_map/reduce_scatter | solution.py:23
  218.2 0.7 copy-start
Sparse Core Ops, SparseCore 0:
  27.4 40.9 all-gather.1
  218.4 43.2 reduce-scatter.1
